TPU v7x, 32 devices: a whole 2x2x4 slice. The times are simulated.
32 devices in a mesh: tm: 4 (over z), chan: 8 (over y, x, core).
Axes of the slice: x: 2, y: 2, z: 4, core: 2. Of those that a mesh axis runs over, the one named last changes fastest.
Arguments:
- voltages: bfloat16 [131072, 2048], P('tm', 'chan'), may hold values from -6 to 6
- band_start: int32 [1], replicated, may hold values from 0 to 992
- feed_map: int32 [2048], replicated, may hold values from 0 to 2047, each once
Outputs:
- visibilities: bfloat16 [32, 2, 2048, 2048], P(('tm', 'chan'))
Inputs may be any that keep to these rules, and one draw needn't show every extreme that they name: feed_map names every input once.
All inputs are finite; a program needn't handle non-finite values.
Results may differ from a plain program's by a relative error of at most 0.0079.
Values may be sent and summed in bfloat16 or wider, within the bound.
A program may use at most 128 MiB of HBM per device.

v0:
```python
import math

import jax
import jax.numpy as jnp
from jax import lax
from jax.sharding import PartitionSpec as P

NFFT = 2048
TAPS = 4
CH_DEV = 1


def from_behind(value, axis, steps):
    count = lax.axis_size(axis)
    first, last = (max(0, -steps), min(count, count - steps))
    return lax.ppermute(value, axis, [(source, source + steps) for source in range(first, last)])


def taps_window():
    total = TAPS * NFFT
    position = jnp.arange(total, dtype=jnp.float32)
    offset = (position - total / 2 + 0.5) / NFFT
    taper = 0.5 - 0.5 * jnp.cos(2.0 * math.pi * (position + 0.5) / total)
    return (jnp.sinc(offset) * taper).reshape(TAPS, NFFT)


def dft_table(start, count):
    samples = jnp.arange(NFFT, dtype=jnp.int32)
    channel = start + jnp.arange(count, dtype=jnp.int32)
    phase = samples[:, None] * channel[None, :] % NFFT
    angle = 2.0 * math.pi * phase.astype(jnp.float32) / NFFT
    scale = 1.0 / math.sqrt(NFFT)
    return (jnp.concatenate([jnp.cos(angle), -jnp.sin(angle)], 1) * scale).astype(jnp.bfloat16)


def on_device(voltages, band_start, feed_map):
    time_count = lax.axis_size("tm")
    input_count = lax.axis_size("chan")
    band_count = CH_DEV * time_count * input_count
    local_inputs = voltages.shape[1]
    frames = voltages.reshape(-1, NFFT, local_inputs)
    spec_count = frames.shape[0]
    earlier = from_behind(frames[spec_count - TAPS + 1 :], "tm", 1)
    extended = jnp.concatenate([earlier, frames], 0)
    window = taps_window()
    total = window[0][None, :, None] * extended[0:spec_count].astype(jnp.float32)
    for tap in range(1, TAPS):
        total = total + window[tap][None, :, None] * extended[tap : tap + spec_count].astype(
            jnp.float32
        )
    weighted = total.astype(jnp.bfloat16)
    table = dft_table(band_start[0], band_count)
    spectra = jnp.einsum("snf,nc->sfc", weighted, table, preferred_element_type=jnp.float32).astype(
        jnp.bfloat16
    )
    turned = spectra.reshape(spec_count, local_inputs, 2, band_count).transpose(3, 2, 0, 1)
    received = lax.all_to_all(turned, ("tm", "chan"), split_axis=0, concat_axis=0, tiled=True)
    blocks = received.reshape(time_count, input_count, CH_DEV, 2, spec_count, local_inputs)
    grids = blocks.transpose(2, 3, 0, 4, 1, 5).reshape(
        CH_DEV, 2, time_count * spec_count, input_count * local_inputs
    )
    ordered = jnp.take(grids, feed_map, axis=3)
    real_part = ordered[:, 0]
    imag_part = ordered[:, 1]
    left_side = jnp.concatenate([real_part, imag_part], 1)
    right_side = jnp.concatenate([imag_part, -real_part], 1)
    cosine_part = jnp.einsum(
        "csf,csg->cfg", left_side, left_side, preferred_element_type=jnp.float32
    )
    sine_part = jnp.einsum(
        "csf,csg->cfg", right_side, left_side, preferred_element_type=jnp.float32
    )
    spectra_total = ordered.shape[2]
    return (jnp.stack([cosine_part, sine_part], 1) / spectra_total).astype(jnp.bfloat16)


def solution(mesh):
    return jax.shard_map(
        on_device,
        mesh=mesh,
        in_specs=(P("tm", "chan"), P(), P()),
        out_specs=P(("tm", "chan"), None, None, None),
        check_vma=False,
    )
```

profile of v0, /device:TPU:0, one launch (start us, length us, event | category | flops | bytes accessed | tf_op | source)
XLA Modules:
  0.0 150.6 jit_solution(282474219122756684)
XLA Ops:
  0.0 2.1 %slice.38 = bf16[6144,256]{1,0:T(8,128)(2,1)S(1)} slice(bf16[32768,256]{1,0:T(8,128)(2,1)} %param.3), slice={[26624:32768], [0:256]} | slice | bytes 6291456 | tf_op jit(solution)/shard_map/slice | solution.py:43
  2.1 5.1 %collective-permute-start = (bf16[3,2048,256]{2,1,0:T(8,128)(2,1)S(1)}, bf16[3,2048,256]{2,1,0:T(8,128)(2,1)S(1)}, u32[]{:S(2)}, u32[]{:S(2)}) collective-permute-start(bf16[3,2048,256]{2,1,0:T(8,128)(2,1)S(1)} %bitcast.38), channel_id=1, source_target_pairs={{0,8},{8,16},{16,24},{1,9},{9,17},{17,25},{2,10},{10,18},{18,26},{... | collective-permute-start | bytes 9437192 | tf_op jit(solution)/shard_map/ppermute | solution.py:16
  7.9 0.2 fusion.22
  8.1 1.1 fusion.17
  9.2 65.2 %collective-permute-done = bf16[3,2048,256]{2,1,0:T(8,128)(2,1)S(1)} collective-permute-done((bf16[3,2048,256]{2,1,0:T(8,128)(2,1)S(1)}, bf16[3,2048,256]{2,1,0:T(8,128)(2,1)S(1)}, u32[]{:S(2)}, u32[]{:S(2)}) %collective-permute-start) | collective-permute-done | bytes 3145760 | tf_op jit(solution)/shard_map/ppermute | solution.py:16
  74.4 0.0 copy-start
  74.4 21.5 %fusion.4 = bf16[16,256,64]{1,2,0:T(8,128)(2,1)S(1)} fusion(bf16[16,2048,256]{2,1,0:T(8,128)(2,1)} %bitcast.40, bf16[3,2048,256]{2,1,0:T(8,128)(2,1)S(1)} %collective-permute-done, f32[2048]{0:T(1024)S(1)} %get-tuple-element.8, f32[2048]{0:T(1024)S(1)} %get-tuple-element.9, f32[2048]{0:T(1024)S(1)} %get-tuple-element.10, f32[2048]{0:T(1024)S(1)} %get-tuple-element.7, ...), kind=kOutput, calls=%fused_computation.15 | convolution fusion | flops 1250557952 | bytes 21004288 | tf_op jit(solution)/shard_map/snf,nc->sfc/dot_general | solution.py:53
  95.9 1.1 copy.18
  97.0 6.8 %all-to-all-start = ((bf16[32,2,16,256]{3,2,1,0:T(8,128)(2,1)}), bf16[32,2,16,256]{3,2,1,0:T(8,128)(2,1)S(1)}, u32[]{:S(2)}, u32[]{:S(2)}) async-start(bf16[32,2,16,256]{3,2,1,0:T(8,128)(2,1)} %bitcast.32), calls=%async_computation | async-start | bytes 1048576 | tf_op jit(solution)/shard_map/all_to_all | solution.py:57
  103.7 0.0 copy-done
  103.8 15.5 %all-to-all-done = bf16[32,2,16,256]{3,2,1,0:T(8,128)(2,1)S(1)} async-done(((bf16[32,2,16,256]{3,2,1,0:T(8,128)(2,1)}), bf16[32,2,16,256]{3,2,1,0:T(8,128)(2,1)S(1)}, u32[]{:S(2)}, u32[]{:S(2)}) %all-to-all-start) | async-done | bytes 524320 | tf_op jit(solution)/shard_map/all_to_all | solution.py:57
  119.3 0.3 copy.13
  119.6 0.2 reshape.113
  119.8 0.8 copy.14
  120.6 7.0 %gather_fusion = bf16[2048,2,64]{2,1,0:T(2,128)(2,1)S(1)} fusion(bf16[2,64,2048]{1,0,2:T(2,128)(2,1)S(1)} %copy.14, s32[2048]{0:T(1024)S(1)} %fusion.47), kind=kCustom, calls=%fused_computation | custom fusion | bytes 1056768 | tf_op jit(solution)/shard_map/jit(_take)/gather | solution.py:62
  127.7 7.5 %broadcast_select_fusion = bf16[1,2,64,2048]{2,1,3,0:T(2,128)(2,1)S(1)} fusion(pred[2048]{0:T(1024)(128)(4,1)S(1)} %compare_and_fusion, bf16[2048,2,64]{2,1,0:T(2,128)(2,1)S(1)} %gather_fusion), kind=kLoop, calls=%fused_computation.14 | loop fusion | flops 262144 | bytes 1050624 | tf_op jit(solution)/shard_map/jit(_take)/select_n | solution.py:62
  135.1 1.5 fusion.53
  136.6 0.6 copy.16
  137.2 0.6 copy.15
  137.9 2.4 %convolution_bitcast_fusion.1 = f32[1,1,2048,2048]{3,2,1,0:T(8,128)S(1)} fusion(bf16[1,64,2048]{2,1,0:T(8,128)(2,1)S(1)} %bitcast.36, bf16[1,64,2048]{2,1,0:T(8,128)(2,1)S(1)} %bitcast.34), kind=kOutput, calls=%fused_computation.13 | convolution fusion | flops 1074790400 | bytes 17301504 | tf_op jit(solution)/shard_map/csf,csg->cfg/dot_general | solution.py:67
  140.2 2.4 %convolution_bitcast_fusion = f32[1,1,2048,2048]{3,2,1,0:T(8,128)S(1)} fusion(bf16[1,64,2048]{2,1,0:T(8,128)(2,1)S(1)} %bitcast_negate_fusion, bf16[1,64,2048]{2,1,0:T(8,128)(2,1)S(1)} %bitcast.37, bf16[1,64,2048]{2,1,0:T(8,128)(2,1)S(1)} %bitcast.35), kind=kOutput, calls=%fused_computation.12 | convolution fusion | flops 1075838976 | bytes 17563648 | tf_op jit(solution)/shard_map/csf,csg->cfg/dot_general | solution.py:70
  142.6 8.0 %fusion = bf16[1,2,2048,2048]{3,2,1,0:T(8,128)(2,1)} fusion(f32[1,1,2048,2048]{3,2,1,0:T(8,128)S(1)} %convolution_bitcast_fusion, f32[1,1,2048,2048]{3,2,1,0:T(8,128)S(1)} %convolution_bitcast_fusion.1), kind=kLoop, calls=%fused_computation.2 | loop fusion | flops 25165824 | bytes 50331648 | tf_op jit(solution)/shard_map/convert_element_type | solution.py:74
  (5 shorter events, 0.0 us)
Async XLA Ops:
  2.1 72.3 %collective-permute-start = (bf16[3,2048,256]{2,1,0:T(8,128)(2,1)S(1)}, bf16[3,2048,256]{2,1,0:T(8,128)(2,1)S(1)}, u32[]{:S(2)}, u32[]{:S(2)}) collective-permute-start(bf16[3,2048,256]{2,1,0:T(8,128)(2,1)S(1)} %bitcast.38), channel_id=1, source_target_pairs={{0,8},{8,16},{16,24},{1,9},{9,17},{17,25},{2,10},{10,18},{18,26},{... | collective-permute-start | bytes 9437192 | tf_op jit(solution)/shard_map/ppermute | solution.py:16
  74.4 29.4 %copy-start = (s32[2048]{0:T(1024)S(1)}, s32[2048]{0:T(1024)}, u32[]{:S(2)}) copy-start(s32[2048]{0:T(1024)} %param.5) | copy-start | bytes 24580
  97.0 22.3 %all-to-all-start = ((bf16[32,2,16,256]{3,2,1,0:T(8,128)(2,1)}), bf16[32,2,16,256]{3,2,1,0:T(8,128)(2,1)S(1)}, u32[]{:S(2)}, u32[]{:S(2)}) async-start(bf16[32,2,16,256]{3,2,1,0:T(8,128)(2,1)} %bitcast.32), calls=%async_computation | async-start | bytes 1048576 | tf_op jit(solution)/shard_map/all_to_all | solution.py:57
where the time goes:
time: 151 us
  waiting for transfers between devices  80.7 us (53%)
  matrix products  26.2 us (17%)
  other arithmetic  16.8 us (11%)
  local copies, waits for them, and re-layouts  14.2 us (9%)
  starting transfers between devices  11.9 us (8%)
    ppermute x1, waiting for transfers between devices, from_behind(): lax.ppermute(value, axis, [(source, source + steps) for source in range(f...  65.2 us
    dot_general x1, matrix products, on_device(): jnp.einsum('snf,nc->sfc', weighted, table, preferred_element_type=jnp.flo...  21.5 us
    all_to_all x1, waiting for transfers between devices, on_device(): lax.all_to_all(turned, ('tm', 'chan'), split_axis=0, concat_axis=0, tiled...  15.5 us
    convert_element_type x1, other arithmetic, on_device(): (jnp.stack([cosine_part, sine_part], 1) / spectra_total).astype(jnp.bfloa...  8.03 us
    select_n x1, other arithmetic, on_device(): ordered = jnp.take(grids, feed_map, axis=3)  7.45 us
    gather x1, local copies, waits for them, and re-layouts, on_device(): ordered = jnp.take(grids, feed_map, axis=3)  7.05 us
    all_to_all x1, starting transfers between devices, on_device(): lax.all_to_all(turned, ('tm', 'chan'), split_axis=0, concat_axis=0, tiled...  6.75 us
    ppermute x1, starting transfers between devices, from_behind(): lax.ppermute(value, axis, [(source, source + steps) for source in range(f...  5.13 us
  transfers between devices with their start and end apart: 2, of which 2 were waited for; matrix products, arithmetic and copies ran while one was open for 1% of the time, Pallas kernels for 0%

commit v1 on v0

v1 whole, which is shorter than its diff:
```python
import functools
import math

import jax
import jax.numpy as jnp
import numpy as np
from jax import lax
from jax.experimental import pallas as pl
from jax.experimental.pallas import tpu as pltpu
from jax.sharding import PartitionSpec as P

NFFT = 2048
TAPS = 4
MESH = pl.DeviceIdType.MESH


def taps_window():
    total = TAPS * NFFT
    position = np.arange(total, dtype=np.float64)
    offset = (position - total / 2 + 0.5) / NFFT
    taper = 0.5 - 0.5 * np.cos(2.0 * math.pi * (position + 0.5) / total)
    return (np.sinc(offset) * taper).reshape(TAPS, NFFT).astype(np.float32)


def base_table(count):
    phase = np.arange(count)[:, None] * np.arange(NFFT)[None, :] % NFFT
    angle = 2.0 * math.pi * phase / NFFT
    scale = 1.0 / math.sqrt(NFFT)
    return np.stack([np.cos(angle) * scale, np.sin(angle) * scale]).astype(np.float32)


def channelize(
    time_count,
    input_count,
    start_ref,
    base_ref,
    window_ref,
    feed_ref,
    volts_ref,
    out_ref,
    volts,
    weights,
    acc,
    carry_out,
    carry_in,
    message,
    received,
    select,
    volts_sem,
    carry_sem,
    send_sem,
    recv_sem,
):
    frames, _, inputs = volts.shape
    count = time_count * input_count
    cols = 2 * count
    half = frames // 2
    tm = lax.axis_index("tm")
    chan = lax.axis_index("chan")
    me = tm * input_count + chan
    keep = TAPS - 1

    def load(frame):
        return pltpu.make_async_copy(
            volts_ref.at[pl.ds(pl.multiple_of(frame * NFFT, NFFT), NFFT), :],
            volts.at[frame],
            volts_sem.at[frame],
        )

    order = list(range(frames - keep, frames)) + list(range(half - keep, frames - keep))
    order += list(range(0, half - keep))
    for frame in order:
        load(frame).start()

    barrier = pltpu.get_barrier_semaphore()

    def greet(step, carry):
        other = lax.rem(me + step, count)
        pl.semaphore_signal(
            barrier,
            inc=1,
            device_id=(other // input_count, lax.rem(other, input_count)),
            device_id_type=MESH,
        )
        return carry

    lax.fori_loop(1, count, greet, 0)

    sample = lax.broadcasted_iota(jnp.int32, (1, NFFT), 1)
    phase = (sample * start_ref[0]) & (NFFT - 1)
    angle = phase.astype(jnp.float32) * (2.0 * math.pi / NFFT)
    turn_cos = jnp.cos(angle)
    turn_sin = jnp.sin(angle)
    base_cos = base_ref[0]
    base_sin = base_ref[1]
    real_rows = base_cos * turn_cos - base_sin * turn_sin
    imag_rows = -(base_sin * turn_cos + base_cos * turn_sin)
    for tap in range(TAPS):
        taper = window_ref[tap : tap + 1, :]
        weights[tap * cols : tap * cols + count, :] = (real_rows * taper).astype(jnp.bfloat16)
        weights[tap * cols + count : (tap + 1) * cols, :] = (imag_rows * taper).astype(jnp.bfloat16)
    acc[...] = jnp.zeros_like(acc)

    def one_frame(frame, carry):
        load(frame).wait()
        result = jnp.dot(weights[...], volts[frame], preferred_element_type=jnp.float32)
        for tap in range(TAPS):
            at = pl.multiple_of((frame + keep - tap) * cols, cols)
            rows = pl.ds(at, cols)
            for lane in range(inputs // 128):
                part = result[tap * cols : (tap + 1) * cols, lane * 128 : (lane + 1) * 128]
                acc[lane, rows, :] = acc[lane, rows, :] + part
        return carry

    lax.fori_loop(frames - keep, frames, one_frame, 0)
    for lane in range(inputs // 128):
        carry_out[:, lane * 128 : (lane + 1) * 128] = acc[lane, frames * cols :, :].astype(
            jnp.bfloat16
        )
    pl.semaphore_wait(barrier, count - 1)

    carry_copy = pltpu.make_async_remote_copy(
        src_ref=carry_out,
        dst_ref=carry_in,
        send_sem=carry_sem.at[0],
        recv_sem=carry_sem.at[1],
        device_id=(lax.rem(tm + 1, time_count), chan),
        device_id_type=MESH,
    )

    @pl.when(tm < time_count - 1)
    def _():
        carry_copy.start()

    def send_half(part):
        def one(step, carry):
            channel = lax.rem(me + step, count)
            first = part * half * cols + channel
            for lane in range(inputs // 128):
                plane = acc.at[lane]
                real = plane[pl.ds(first, half, stride=cols), :]
                imag = plane[pl.ds(first + count, half, stride=cols), :]
                message[part, channel, :, lane * 128 : (lane + 1) * 128] = jnp.concatenate(
                    [real, imag], 0
                ).astype(jnp.bfloat16)

            @pl.when(step < count)
            def _():
                pltpu.make_async_remote_copy(
                    src_ref=message.at[part, channel],
                    dst_ref=received.at[part, chan, tm],
                    send_sem=send_sem.at[part],
                    recv_sem=recv_sem.at[part],
                    device_id=(channel // input_count, lax.rem(channel, input_count)),
                    device_id_type=MESH,
                ).start()

            @pl.when(step == count)
            def _():
                pltpu.make_async_copy(
                    message.at[part, channel], received.at[part, chan, tm], recv_sem.at[part]
                ).start()

            return carry

        lax.fori_loop(1, count + 1, one, 0)

    lax.fori_loop(half - keep, frames - keep, one_frame, 0)
    send_half(1)
    lax.fori_loop(0, half - keep, one_frame, 0)

    @pl.when(tm > 0)
    def _():
        carry_copy.wait_recv()
        for lane in range(inputs // 128):
            before = carry_in[:, lane * 128 : (lane + 1) * 128].astype(jnp.float32)
            acc[lane, : keep * cols, :] = acc[lane, : keep * cols, :] + before

    send_half(0)

    total = input_count * inputs
    block = 256

    def one_select(index, carry):
        at = pl.multiple_of(index * block, block)
        rows = lax.broadcasted_iota(jnp.int32, (block, total), 0) + at
        select[pl.ds(at, block), :] = jnp.where(rows == feed_ref[...], 1.0, 0.0).astype(
            jnp.bfloat16
        )
        return carry

    lax.fori_loop(0, total // block, one_select, 0)

    tall = time_count * 2 * half
    for part in (1, 0):
        pltpu.make_async_copy(received.at[part], received.at[part], recv_sem.at[part]).wait()
        grid = jnp.concatenate(
            [received[part, at].reshape(tall, inputs) for at in range(input_count)], 1
        )

        def one_order(index, carry):
            at = pl.multiple_of(index * block, block)
            out_ref[part * tall : (part + 1) * tall, pl.ds(at, block)] = jnp.dot(
                grid, select[:, pl.ds(at, block)], preferred_element_type=jnp.float32
            ).astype(jnp.bfloat16)
            return carry

        lax.fori_loop(0, total // block, one_order, 0)

    for part in range(2):
        sent = message.at[part, pl.ds(0, count - 1)]
        pltpu.make_async_copy(sent, sent, send_sem.at[part]).wait()

    @pl.when(tm < time_count - 1)
    def _():
        carry_copy.wait_send()


def correlate(half, scale, ordered_ref, out_ref):
    rows = out_ref.shape[2]
    tall = ordered_ref.shape[0]
    at = pl.multiple_of(pl.program_id(0) * rows, rows)
    side = ordered_ref[:, pl.ds(at, rows)].astype(jnp.float32) * scale
    pairs = side.reshape(tall // (2 * half), 2, half, rows)
    turned = jnp.stack([pairs[:, 1], -pairs[:, 0]], 1).reshape(tall, rows)
    for part, left in enumerate((side, turned)):
        out_ref[0, part] = jnp.dot(
            left.T.astype(jnp.bfloat16), ordered_ref[...], preferred_element_type=jnp.float32
        ).astype(jnp.bfloat16)


def on_device(voltages, band_start, feed_map):
    time_count = lax.axis_size("tm")
    input_count = lax.axis_size("chan")
    count = time_count * input_count
    samples, inputs = voltages.shape
    frames = samples // NFFT
    total = input_count * inputs
    cols = 2 * count
    half = frames // 2
    spectra = time_count * frames
    bf16 = jnp.bfloat16
    vmem = pl.BlockSpec(memory_space=pltpu.VMEM)
    keep = TAPS - 1
    ordered = pl.pallas_call(
        functools.partial(channelize, time_count, input_count),
        out_shape=jax.ShapeDtypeStruct((2 * spectra, total), bf16),
        in_specs=[
            pl.BlockSpec(memory_space=pltpu.SMEM),
            vmem,
            vmem,
            vmem,
            pl.BlockSpec(memory_space=pl.ANY),
        ],
        out_specs=vmem,
        scratch_shapes=[
            pltpu.VMEM((frames, NFFT, inputs), bf16),
            pltpu.VMEM((TAPS * cols, NFFT), bf16),
            pltpu.VMEM((inputs // 128, (frames + keep) * cols, 128), jnp.float32),
            pltpu.VMEM((keep * cols, inputs), bf16),
            pltpu.VMEM((keep * cols, inputs), bf16),
            pltpu.VMEM((2, count, 2 * half, inputs), bf16),
            pltpu.VMEM((2, input_count, time_count, 2 * half, inputs), bf16),
            pltpu.VMEM((total, total), bf16),
            pltpu.SemaphoreType.DMA((frames,)),
            pltpu.SemaphoreType.DMA((2,)),
            pltpu.SemaphoreType.DMA((2,)),
            pltpu.SemaphoreType.DMA((2,)),
        ],
        compiler_params=pltpu.CompilerParams(
            collective_id=0, has_side_effects=True, vmem_limit_bytes=50 * 2**20
        ),
        cost_estimate=pl.CostEstimate(
            flops=2 * samples * inputs * TAPS * cols,
            bytes_accessed=samples * inputs * 2,
            transcendentals=0,
        ),
        name="channelize",
    )(
        band_start,
        jnp.asarray(base_table(count)),
        jnp.asarray(taps_window()),
        feed_map.reshape(1, total),
        voltages,
    )
    rows = 256
    return pl.pallas_call(
        functools.partial(correlate, half, 1.0 / spectra),
        grid=(total // rows,),
        out_shape=jax.ShapeDtypeStruct((1, 2, total, total), bf16),
        in_specs=[pl.BlockSpec((2 * spectra, total), lambda i: (0, 0))],
        out_specs=pl.BlockSpec((1, 2, rows, total), lambda i: (0, 0, i, 0)),
        compiler_params=pltpu.CompilerParams(vmem_limit_bytes=50 * 2**20),
        cost_estimate=pl.CostEstimate(
            flops=8 * spectra * total * total,
            bytes_accessed=4 * total * total,
            transcendentals=0,
        ),
        name="correlate",
    )(ordered)


def solution(mesh):
    return jax.shard_map(
        on_device,
        mesh=mesh,
        in_specs=(P("tm", "chan"), P(), P()),
        out_specs=P(("tm", "chan"), None, None, None),
        check_vma=False,
    )
```

time: 151 us -> 37.6 us (0.25)
  waiting for transfers between devices: 80.7 us -> 0 us
  Pallas kernels: 0 us -> 34.2 us
  matrix products: 26.2 us -> 0 us
  other arithmetic: 16.8 us -> 0 us
  starting transfers between devices: 11.9 us -> 0 us
  local copies, waits for them, and re-layouts: 14.2 us -> 2.49 us
    ppermute x1 -> x0, waiting for transfers between devices: 65.2 us -> none  [from_behind(): lax.ppermute(value, axis, [(source, source + steps) for source in range(f...]
    pallas_call x0 -> x2, Pallas kernels: none -> 34.2 us  [the longest x1 25.1 us: on_device(): pl.pallas_call(functools.partial(channelize, time_count, input_count), ou...]
    dot_general x3 -> x0, matrix products: 26.2 us -> none  [the longest x1 21.5 us: on_device(): jnp.einsum('snf,nc->sfc', weighted, table, preferred_element_type=jnp.flo...]
    all_to_all x1 -> x0, waiting for transfers between devices: 15.5 us -> none  [on_device(): lax.all_to_all(turned, ('tm', 'chan'), split_axis=0, concat_axis=0, tiled...]
    convert_element_type x1 -> x0, other arithmetic: 8.03 us -> none  [on_device(): (jnp.stack([cosine_part, sine_part], 1) / spectra_total).astype(jnp.bfloa...]
    select_n x1 -> x0, other arithmetic: 7.45 us -> none  [on_device(): ordered = jnp.take(grids, feed_map, axis=3)]
    gather x1 -> x0, local copies, waits for them, and re-layouts: 7.05 us -> none  [on_device(): ordered = jnp.take(grids, feed_map, axis=3)]
    all_to_all x1 -> x0, starting transfers between devices: 6.75 us -> none  [on_device(): lax.all_to_all(turned, ('tm', 'chan'), split_axis=0, concat_axis=0, tiled...]
  transfers between devices with their start and end apart: 2 -> 0, of which waited for: 2 -> 0; matrix products, arithmetic and copies ran while one was open for 1% -> 0% of each run, Pallas kernels for 0% -> 0%
where the time goes in v1:
time: 37.6 us; the launch traced here: 37.3 us
  Pallas kernels  34.2 us (91%)
  local copies, waits for them, and re-layouts  2.49 us (7%)
  between operations  0.67 us (2%)
    pallas_call x1, Pallas kernels, on_device(): pl.pallas_call(functools.partial(channelize, time_count, input_count), ou...  25.1 us
    pallas_call x1, Pallas kernels, on_device(): pl.pallas_call(functools.partial(correlate, half, 1.0 / spectra), grid=(t...  9.07 us
    unnamed x6, local copies, waits for them, and re-layouts  2.49 us

profile of v1, /device:TPU:0, one launch (start us, length us, event | category | flops | bytes accessed | tf_op | source)
XLA Modules:
  0.0 37.3 jit_solution(17558894722400623425)
XLA Ops:
  0.7 0.0 copy-start
  0.7 1.0 %copy-done = f32[2,32,2048]{2,1,0:T(8,128)S(1)} copy-done((f32[2,32,2048]{2,1,0:T(8,128)S(1)}, f32[2,32,2048]{2,1,0:T(8,128)}, u32[]{:S(2)}) %copy-start) | copy-done | bytes 524312
  1.7 0.0 copy-start.1
  1.7 0.8 %copy-done.1 = f32[4,2048]{1,0:T(4,128)S(1)} copy-done((f32[4,2048]{1,0:T(4,128)S(1)}, f32[4,2048]{1,0:T(4,128)}, u32[]{:S(2)}) %copy-start.1) | copy-done | bytes 32792
  2.5 0.0 copy-start.2
  2.5 0.7 %copy-done.2 = s32[2048]{0:T(1024)S(1)} copy-done((s32[2048]{0:T(1024)S(1)}, s32[2048]{0:T(1024)}, u32[]{:S(2)}) %copy-start.2) | copy-done | bytes 8216
  3.2 25.1 %channelize.1.ordered_ref = bf16[128,2048]{1,0:T(8,128)(2,1)S(1)} custom-call(s32[1]{0:T(128)S(6)} %copy.6.start_ref, f32[2,32,2048]{2,1,0:T(8,128)S(1)} %copy-done, f32[4,2048]{1,0:T(4,128)S(1)} %copy-done.1, s32[1,2048]{1,0:T(1,128)S(1)} %bitcast.1, bf16[32768,256]{1,0:T(8,128)(2,1)} %volts_ref.1), custom_call_target="tpu_custom_call" | custom-call | flops 4294967296 | bytes 16777216 | tf_op jit(solution)/shard_map/channelize/pallas_call | solution.py:245
  28.3 9.1 %correlate.1 = bf16[1,2,2048,2048]{3,2,1,0:T(8,128)(2,1)} custom-call(bf16[128,2048]{1,0:T(8,128)(2,1)S(1)} %channelize.1.ordered_ref), custom_call_target="tpu_custom_call" | custom-call | flops 2147483648 | bytes 16777216 | tf_op jit(solution)/shard_map/correlate/pallas_call | solution.py:287
Async XLA Ops:
  0.7 1.0 %copy-start = (f32[2,32,2048]{2,1,0:T(8,128)S(1)}, f32[2,32,2048]{2,1,0:T(8,128)}, u32[]{:S(2)}) copy-start(f32[2,32,2048]{2,1,0:T(8,128)} %constant.4.clone.base_ref) | copy-start | bytes 1572868
  1.7 0.8 %copy-start.1 = (f32[4,2048]{1,0:T(4,128)S(1)}, f32[4,2048]{1,0:T(4,128)}, u32[]{:S(2)}) copy-start(f32[4,2048]{1,0:T(4,128)} %constant.5.clone.window_ref) | copy-start | bytes 98308
  2.5 0.7 %copy-start.2 = (s32[2048]{0:T(1024)S(1)}, s32[2048]{0:T(1024)}, u32[]{:S(2)}) copy-start(s32[2048]{0:T(1024)} %param.7) | copy-start | bytes 24580

commit v2 on v1

v2 whole, which is shorter than its diff:
```python
import functools
import math

import jax
import jax.numpy as jnp
import numpy as np
from jax import lax
from jax.experimental import pallas as pl
from jax.experimental.pallas import tpu as pltpu
from jax.sharding import PartitionSpec as P

NFFT = 2048
TAPS = 4
MESH = pl.DeviceIdType.MESH


def taps_window():
    total = TAPS * NFFT
    position = np.arange(total, dtype=np.float64)
    offset = (position - total / 2 + 0.5) / NFFT
    taper = 0.5 - 0.5 * np.cos(2.0 * math.pi * (position + 0.5) / total)
    return (np.sinc(offset) * taper).reshape(TAPS, NFFT).astype(np.float32)


def base_table(count):
    phase = np.arange(count)[:, None] * np.arange(NFFT)[None, :] % NFFT
    angle = 2.0 * math.pi * phase / NFFT
    scale = 1.0 / math.sqrt(NFFT)
    return np.stack([np.cos(angle) * scale, np.sin(angle) * scale]).astype(np.float32)


def channelize(
    time_count,
    input_count,
    start_ref,
    base_hbm,
    window_hbm,
    feed_hbm,
    volts_ref,
    out_ref,
    base_ref,
    window_ref,
    feed_ref,
    volts,
    weights,
    acc,
    carry_out,
    carry_in,
    message,
    received,
    select,
    total_acc,
    const_sem,
    volts_sem,
    carry_sem,
    send_sem,
    recv_sem,
):
    frames, _, inputs = volts.shape
    count = time_count * input_count
    cols = 2 * count
    lanes = inputs // 128
    piece = 8 // lanes
    pieces = frames // piece
    tm = lax.axis_index("tm")
    chan = lax.axis_index("chan")
    me = tm * input_count + chan
    keep = TAPS - 1

    def load(frame):
        return pltpu.make_async_copy(
            volts_ref.at[pl.ds(pl.multiple_of(frame * NFFT, NFFT), NFFT), :],
            volts.at[frame],
            volts_sem.at[frame],
        )

    consts = [
        pltpu.make_async_copy(source, target, const_sem.at[index])
        for index, (source, target) in enumerate(
            ((base_hbm, base_ref), (window_hbm, window_ref), (feed_hbm, feed_ref))
        )
    ]
    for copy in consts:
        copy.start()
    for frame in range(frames - keep, frames):
        load(frame).start()

    barrier = pltpu.get_barrier_semaphore()

    def greet(step, carry):
        other = lax.rem(me + step, count)
        pl.semaphore_signal(
            barrier,
            inc=1,
            device_id=(other // input_count, lax.rem(other, input_count)),
            device_id_type=MESH,
        )
        return carry

    lax.fori_loop(1, count, greet, 0)

    sample = lax.broadcasted_iota(jnp.int32, (1, NFFT), 1)
    phase = (sample * start_ref[0]) & (NFFT - 1)
    angle = phase.astype(jnp.float32) * (2.0 * math.pi / NFFT)
    turn_cos = jnp.cos(angle)
    turn_sin = jnp.sin(angle)
    consts[0].wait()
    consts[1].wait()
    for frame in reversed(range(0, frames - keep)):
        load(frame).start()
    base_cos = base_ref[0]
    base_sin = base_ref[1]
    real_rows = base_cos * turn_cos - base_sin * turn_sin
    imag_rows = -(base_sin * turn_cos + base_cos * turn_sin)
    for tap in range(TAPS):
        taper = window_ref[tap : tap + 1, :]
        weights[tap * cols : tap * cols + count, :] = (real_rows * taper).astype(jnp.bfloat16)
        weights[tap * cols + count : (tap + 1) * cols, :] = (imag_rows * taper).astype(jnp.bfloat16)
    acc[...] = jnp.zeros_like(acc)

    total = input_count * inputs
    block = 256

    def some_frames(first, number):
        for index in range(number):
            load(first + index).wait()
        for index in range(number):
            frame = first + index
            result = jnp.dot(weights[...], volts[frame], preferred_element_type=jnp.float32)
            for tap in range(TAPS):
                rows = pl.ds(pl.multiple_of((frame + keep - tap) * cols, cols), cols)
                for lane in range(lanes):
                    part = result[tap * cols : (tap + 1) * cols, lane * 128 : (lane + 1) * 128]
                    acc[lane, rows, :] = acc[lane, rows, :] + part

    some_frames(frames - keep, keep)
    for lane in range(inputs // 128):
        carry_out[:, lane * 128 : (lane + 1) * 128] = acc[lane, frames * cols :, :].astype(
            jnp.bfloat16
        )
    pl.semaphore_wait(barrier, count - 1)

    carry_copy = pltpu.make_async_remote_copy(
        src_ref=carry_out,
        dst_ref=carry_in,
        send_sem=carry_sem.at[0],
        recv_sem=carry_sem.at[1],
        device_id=(lax.rem(tm + 1, time_count), chan),
        device_id_type=MESH,
    )

    @pl.when(tm < time_count - 1)
    def _():
        carry_copy.start()

    def send_piece(index):
        def one(step, carry):
            to_chan = lax.rem(chan + step // time_count, input_count)
            to_time = lax.rem(tm + 1 + lax.rem(step, time_count), time_count)
            channel = to_time * input_count + to_chan
            first = index * piece * cols + channel
            rows = [acc.at[lane][pl.ds(first, 2 * piece, stride=count), :] for lane in range(lanes)]
            message[channel, index] = jnp.concatenate(rows, 0).astype(jnp.bfloat16)

            @pl.when(channel != me)
            def _():
                pltpu.make_async_remote_copy(
                    src_ref=message.at[channel, index],
                    dst_ref=received.at[chan, index, tm],
                    send_sem=send_sem,
                    recv_sem=recv_sem.at[chan],
                    device_id=(to_time, to_chan),
                    device_id_type=MESH,
                ).start()

            @pl.when(channel == me)
            def _():
                pltpu.make_async_copy(
                    message.at[channel, index], received.at[chan, index, tm], recv_sem.at[chan]
                ).start()

            return carry

        lax.fori_loop(0, count, one, 0)

    def one_piece(step, carry):
        index = pieces - 1 - step
        some_frames(index * piece - keep, piece)
        send_piece(index)
        return carry

    lax.fori_loop(0, pieces - 1, one_piece, 0)
    some_frames(0, piece - keep)

    @pl.when(tm > 0)
    def _():
        carry_copy.wait_recv()
        for lane in range(lanes):
            before = carry_in[:, lane * 128 : (lane + 1) * 128].astype(jnp.float32)
            acc[lane, : keep * cols, :] = acc[lane, : keep * cols, :] + before

    send_piece(0)

    consts[2].wait()

    def one_select(index, carry):
        at = pl.multiple_of(index * block, block)
        rows = lax.broadcasted_iota(jnp.int32, (block, total), 0) + at
        select[pl.ds(at, block), :] = jnp.where(rows == feed_ref[...], 1.0, 0.0).astype(
            jnp.bfloat16
        )
        return carry

    lax.fori_loop(0, total // block, one_select, 0)

    tall = time_count * 2 * frames
    total_acc[...] = jnp.zeros_like(total_acc)
    wide = 512

    def one_source(step, carry):
        source = lax.rem(chan - step + input_count, input_count)
        landed = received.at[source]
        pltpu.make_async_copy(landed, landed, recv_sem.at[source]).wait()
        grid = received[source].astype(jnp.float32)
        grid = grid.reshape(pieces * time_count, lanes, 2 * piece, 128)
        grid = jnp.concatenate([grid[:, lane] for lane in range(lanes)], 2)
        grid = grid.reshape(tall, inputs).astype(jnp.bfloat16)
        own_rows = pl.ds(pl.multiple_of(source * inputs, inputs), inputs)

        def one_order(index, carry):
            at = pl.ds(pl.multiple_of(index * wide, wide), wide)
            total_acc[:, at] = total_acc[:, at] + jnp.dot(
                grid, select[own_rows, at], preferred_element_type=jnp.float32
            )
            return carry

        lax.fori_loop(0, total // wide, one_order, 0)
        return carry

    lax.fori_loop(0, input_count, one_source, 0)
    out_ref[...] = total_acc[...].astype(jnp.bfloat16)

    sent = message.at[pl.ds(0, count - 1)]
    pltpu.make_async_copy(sent, sent, send_sem).wait()

    @pl.when(tm < time_count - 1)
    def _():
        carry_copy.wait_send()


def correlate(scale, ordered_ref, out_ref):
    rows, total = out_ref.shape[2:]
    tall = ordered_ref.shape[0]
    at = pl.multiple_of(pl.program_id(0) * rows, rows)
    side = ordered_ref[:, pl.ds(at, rows)].astype(jnp.float32) * scale
    row = lax.broadcasted_iota(jnp.int32, (tall, rows), 0)
    turned = jnp.where(
        (row & 1) == 0, pltpu.roll(side, tall - 1, 0), -pltpu.roll(side, 1, 0)
    )
    left = jnp.concatenate([side, turned], 1).astype(jnp.bfloat16)
    both = lax.dot_general(
        left, ordered_ref[...], (((0,), (0,)), ((), ())), preferred_element_type=jnp.float32
    )
    out_ref[0] = both.astype(jnp.bfloat16).reshape(2, rows, total)


def on_device(voltages, band_start, feed_map):
    time_count = lax.axis_size("tm")
    input_count = lax.axis_size("chan")
    count = time_count * input_count
    samples, inputs = voltages.shape
    frames = samples // NFFT
    total = input_count * inputs
    cols = 2 * count
    pieces = frames * inputs // 1024
    spectra = time_count * frames
    bf16 = jnp.bfloat16
    vmem = pl.BlockSpec(memory_space=pltpu.VMEM)
    keep = TAPS - 1
    ordered = pl.pallas_call(
        functools.partial(channelize, time_count, input_count),
        out_shape=jax.ShapeDtypeStruct((2 * spectra, total), bf16),
        in_specs=[pl.BlockSpec(memory_space=pltpu.SMEM)] + [pl.BlockSpec(memory_space=pl.ANY)] * 4,
        out_specs=vmem,
        scratch_shapes=[
            pltpu.VMEM((2, count, NFFT), jnp.float32),
            pltpu.VMEM((TAPS, NFFT), jnp.float32),
            pltpu.VMEM((1, total), jnp.int32),
            pltpu.VMEM((frames, NFFT, inputs), bf16),
            pltpu.VMEM((TAPS * cols, NFFT), bf16),
            pltpu.VMEM((inputs // 128, (frames + keep) * cols, 128), jnp.float32),
            pltpu.VMEM((keep * cols, inputs), bf16),
            pltpu.VMEM((keep * cols, inputs), bf16),
            pltpu.VMEM((count, pieces, 16, 128), bf16),
            pltpu.VMEM((input_count, pieces, time_count, 16, 128), bf16),
            pltpu.VMEM((total, total), bf16),
            pltpu.VMEM((2 * spectra, total), jnp.float32),
            pltpu.SemaphoreType.DMA((3,)),
            pltpu.SemaphoreType.DMA((frames,)),
            pltpu.SemaphoreType.DMA((2,)),
            pltpu.SemaphoreType.DMA,
            pltpu.SemaphoreType.DMA((input_count,)),
        ],
        compiler_params=pltpu.CompilerParams(
            collective_id=0, has_side_effects=True, vmem_limit_bytes=60 * 2**20
        ),
        cost_estimate=pl.CostEstimate(
            flops=2 * samples * inputs * TAPS * cols,
            bytes_accessed=samples * inputs * 2,
            transcendentals=0,
        ),
        name="channelize",
    )(
        band_start,
        jnp.asarray(base_table(count)),
        jnp.asarray(taps_window()),
        feed_map.reshape(1, total),
        voltages,
    )
    rows = 512
    return pl.pallas_call(
        functools.partial(correlate, 1.0 / spectra),
        grid=(total // rows,),
        out_shape=jax.ShapeDtypeStruct((1, 2, total, total), bf16),
        in_specs=[pl.BlockSpec((2 * spectra, total), lambda i: (0, 0))],
        out_specs=pl.BlockSpec((1, 2, rows, total), lambda i: (0, 0, i, 0)),
        compiler_params=pltpu.CompilerParams(vmem_limit_bytes=60 * 2**20),
        cost_estimate=pl.CostEstimate(
            flops=8 * spectra * total * total,
            bytes_accessed=4 * total * total,
            transcendentals=0,
        ),
        name="correlate",
    )(ordered)


def solution(mesh):
    return jax.shard_map(
        on_device,
        mesh=mesh,
        in_specs=(P("tm", "chan"), P(), P()),
        out_specs=P(("tm", "chan"), None, None, None),
        check_vma=False,
    )
```

time: 37.6 us -> 38.2 us (1.016)
  Pallas kernels: 34.2 us -> 37.3 us
  local copies, waits for them, and re-layouts: 2.49 us -> 0 us
    pallas_call x1, Pallas kernels: 25.1 us -> 28.3 us  [on_device(): pl.pallas_call(functools.partial(channelize, time_count, input_count), ou...]
    unnamed x6 -> x0, local copies, waits for them, and re-layouts: 2.49 us -> none
where the time goes in v2:
time: 38.2 us; the launch traced here: 38 us
  Pallas kernels  37.3 us (98%)
  between operations  0.66 us (2%)
    pallas_call x1, Pallas kernels, on_device(): pl.pallas_call(functools.partial(channelize, time_count, input_count), ou...  28.3 us
    pallas_call x1, Pallas kernels, on_device(): pl.pallas_call(functools.partial(correlate, 1.0 / spectra), grid=(total /...  9.06 us

profile of v2, /device:TPU:0, one launch (start us, length us, event | category | flops | bytes accessed | tf_op | source)
XLA Modules:
  0.0 38.0 jit_solution(13641201949835047330)
XLA Ops:
  0.7 28.3 %channelize.1.ordered_ref = bf16[128,2048]{1,0:T(8,128)(2,1)} custom-call(s32[1]{0:T(128)S(6)} %copy.6.start_ref, f32[2,32,2048]{2,1,0:T(8,128)} %constant.4.clone.base_hbm, f32[4,2048]{1,0:T(4,128)} %constant.5.clone.window_hbm, s32[1,2048]{1,0:T(1,128)} %bitcast.1, bf16[32768,256]{1,0:T(8,128)(2,1)} %volts_ref.1), custom_call_target="tpu_custom_call" | custom-call | flops 4294967296 | bytes 16777216 | tf_op jit(solution)/shard_map/channelize/pallas_call | solution.py:280
  28.9 9.1 %correlate.1 = bf16[1,2,2048,2048]{3,2,1,0:T(8,128)(2,1)} custom-call(bf16[128,2048]{1,0:T(8,128)(2,1)} %channelize.1.ordered_ref), custom_call_target="tpu_custom_call" | custom-call | flops 2147483648 | bytes 16777216 | tf_op jit(solution)/shard_map/correlate/pallas_call | solution.py:321

commit v3 on v1

--- a/solution.py
+++ b/solution.py
@@ -33,11 +33,14 @@
     time_count,
     input_count,
     start_ref,
+    base_hbm,
+    window_hbm,
+    feed_hbm,
+    volts_ref,
+    out_ref,
     base_ref,
     window_ref,
     feed_ref,
-    volts_ref,
-    out_ref,
     volts,
     weights,
     acc,
@@ -46,6 +49,7 @@
     message,
     received,
     select,
+    const_sem,
     volts_sem,
     carry_sem,
     send_sem,
@@ -67,6 +71,14 @@
             volts_sem.at[frame],
         )
 
+    consts = [
+        pltpu.make_async_copy(source, target, const_sem.at[index])
+        for index, (source, target) in enumerate(
+            ((base_hbm, base_ref), (window_hbm, window_ref), (feed_hbm, feed_ref))
+        )
+    ]
+    for copy in consts:
+        copy.start()
     order = list(range(frames - keep, frames)) + list(range(half - keep, frames - keep))
     order += list(range(0, half - keep))
     for frame in order:
@@ -91,6 +103,8 @@
     angle = phase.astype(jnp.float32) * (2.0 * math.pi / NFFT)
     turn_cos = jnp.cos(angle)
     turn_sin = jnp.sin(angle)
+    consts[0].wait()
+    consts[1].wait()
     base_cos = base_ref[0]
     base_sin = base_ref[1]
     real_rows = base_cos * turn_cos - base_sin * turn_sin
@@ -101,18 +115,23 @@
         weights[tap * cols + count : (tap + 1) * cols, :] = (imag_rows * taper).astype(jnp.bfloat16)
     acc[...] = jnp.zeros_like(acc)
 
-    def one_frame(frame, carry):
-        load(frame).wait()
-        result = jnp.dot(weights[...], volts[frame], preferred_element_type=jnp.float32)
-        for tap in range(TAPS):
-            at = pl.multiple_of((frame + keep - tap) * cols, cols)
-            rows = pl.ds(at, cols)
-            for lane in range(inputs // 128):
-                part = result[tap * cols : (tap + 1) * cols, lane * 128 : (lane + 1) * 128]
-                acc[lane, rows, :] = acc[lane, rows, :] + part
-        return carry
-
-    lax.fori_loop(frames - keep, frames, one_frame, 0)
+    total = input_count * inputs
+    block = 256
+    lanes = inputs // 128
+
+    def some_frames(first, number):
+        for index in range(number):
+            load(first + index).wait()
+        for index in range(number):
+            frame = first + index
+            result = jnp.dot(weights[...], volts[frame], preferred_element_type=jnp.float32)
+            for tap in range(TAPS):
+                rows = pl.ds(pl.multiple_of((frame + keep - tap) * cols, cols), cols)
+                for lane in range(lanes):
+                    part = result[tap * cols : (tap + 1) * cols, lane * 128 : (lane + 1) * 128]
+                    acc[lane, rows, :] = acc[lane, rows, :] + part
+
+    some_frames(frames - keep, keep)
     for lane in range(inputs // 128):
         carry_out[:, lane * 128 : (lane + 1) * 128] = acc[lane, frames * cols :, :].astype(
             jnp.bfloat16
@@ -165,9 +184,15 @@
 
         lax.fori_loop(1, count + 1, one, 0)
 
-    lax.fori_loop(half - keep, frames - keep, one_frame, 0)
+    group = half // 2
+
+    def one_group(index, carry):
+        some_frames(half - keep + index * group, group)
+        return carry
+
+    lax.fori_loop(0, half // group, one_group, 0)
     send_half(1)
-    lax.fori_loop(0, half - keep, one_frame, 0)
+    some_frames(0, half - keep)
 
     @pl.when(tm > 0)
     def _():
@@ -178,8 +203,7 @@
 
     send_half(0)
 
-    total = input_count * inputs
-    block = 256
+    consts[2].wait()
 
     def one_select(index, carry):
         at = pl.multiple_of(index * block, block)
@@ -200,9 +224,11 @@
 
         def one_order(index, carry):
             at = pl.multiple_of(index * block, block)
-            out_ref[part * tall : (part + 1) * tall, pl.ds(at, block)] = jnp.dot(
+            rows = slice(part * tall, (part + 1) * tall)
+            side = jnp.dot(
                 grid, select[:, pl.ds(at, block)], preferred_element_type=jnp.float32
-            ).astype(jnp.bfloat16)
+            )
+            out_ref[rows, pl.ds(at, block)] = side.astype(jnp.bfloat16)
             return carry
 
         lax.fori_loop(0, total // block, one_order, 0)
@@ -217,16 +243,17 @@
 
 
 def correlate(half, scale, ordered_ref, out_ref):
-    rows = out_ref.shape[2]
+    rows, total = out_ref.shape[2:]
     tall = ordered_ref.shape[0]
     at = pl.multiple_of(pl.program_id(0) * rows, rows)
     side = ordered_ref[:, pl.ds(at, rows)].astype(jnp.float32) * scale
     pairs = side.reshape(tall // (2 * half), 2, half, rows)
     turned = jnp.stack([pairs[:, 1], -pairs[:, 0]], 1).reshape(tall, rows)
-    for part, left in enumerate((side, turned)):
-        out_ref[0, part] = jnp.dot(
-            left.T.astype(jnp.bfloat16), ordered_ref[...], preferred_element_type=jnp.float32
-        ).astype(jnp.bfloat16)
+    left = jnp.concatenate([side, turned], 1).astype(jnp.bfloat16)
+    both = lax.dot_general(
+        left, ordered_ref[...], (((0,), (0,)), ((), ())), preferred_element_type=jnp.float32
+    )
+    out_ref[0] = both.astype(jnp.bfloat16).reshape(2, rows, total)
 
 
 def on_device(voltages, band_start, feed_map):
@@ -245,15 +272,12 @@
     ordered = pl.pallas_call(
         functools.partial(channelize, time_count, input_count),
         out_shape=jax.ShapeDtypeStruct((2 * spectra, total), bf16),
-        in_specs=[
-            pl.BlockSpec(memory_space=pltpu.SMEM),
-            vmem,
-            vmem,
-            vmem,
-            pl.BlockSpec(memory_space=pl.ANY),
-        ],
+        in_specs=[pl.BlockSpec(memory_space=pltpu.SMEM)] + [pl.BlockSpec(memory_space=pl.ANY)] * 4,
         out_specs=vmem,
         scratch_shapes=[
+            pltpu.VMEM((2, count, NFFT), jnp.float32),
+            pltpu.VMEM((TAPS, NFFT), jnp.float32),
+            pltpu.VMEM((1, total), jnp.int32),
             pltpu.VMEM((frames, NFFT, inputs), bf16),
             pltpu.VMEM((TAPS * cols, NFFT), bf16),
             pltpu.VMEM((inputs // 128, (frames + keep) * cols, 128), jnp.float32),
@@ -262,6 +286,7 @@
             pltpu.VMEM((2, count, 2 * half, inputs), bf16),
             pltpu.VMEM((2, input_count, time_count, 2 * half, inputs), bf16),
             pltpu.VMEM((total, total), bf16),
+            pltpu.SemaphoreType.DMA((3,)),
             pltpu.SemaphoreType.DMA((frames,)),
             pltpu.SemaphoreType.DMA((2,)),
             pltpu.SemaphoreType.DMA((2,)),
@@ -283,7 +308,7 @@
         feed_map.reshape(1, total),
         voltages,
     )
-    rows = 256
+    rows = 512
     return pl.pallas_call(
         functools.partial(correlate, half, 1.0 / spectra),
         grid=(total // rows,),

time: 37.6 us -> 36.2 us (0.963)
  Pallas kernels: 34.2 us -> 32.8 us
    pallas_call x1, Pallas kernels: 9.07 us -> 8 us  [on_device(): pl.pallas_call(functools.partial(correlate, half, 1.0 / spectra), grid=(t...]
where the time goes in v3:
time: 36.2 us; the launch traced here: 36 us
  Pallas kernels  32.8 us (91%)
  local copies, waits for them, and re-layouts  2.49 us (7%)
  between operations  0.67 us (2%)
    pallas_call x1, Pallas kernels, on_device(): pl.pallas_call(functools.partial(channelize, time_count, input_count), ou...  24.8 us
    pallas_call x1, Pallas kernels, on_device(): pl.pallas_call(functools.partial(correlate, half, 1.0 / spectra), grid=(t...  8 us
    unnamed x6, local copies, waits for them, and re-layouts  2.49 us

profile of v3, /device:TPU:0, one launch (start us, length us, event | category | flops | bytes accessed | tf_op | source)
XLA Modules:
  0.0 36.0 jit_solution(886613742340920664)
XLA Ops:
  0.7 0.0 copy-start
  0.7 1.0 %copy-done = f32[2,32,2048]{2,1,0:T(8,128)S(1)} copy-done((f32[2,32,2048]{2,1,0:T(8,128)S(1)}, f32[2,32,2048]{2,1,0:T(8,128)}, u32[]{:S(2)}) %copy-start) | copy-done | bytes 524312
  1.7 0.0 copy-start.1
  1.7 0.8 %copy-done.1 = f32[4,2048]{1,0:T(4,128)S(1)} copy-done((f32[4,2048]{1,0:T(4,128)S(1)}, f32[4,2048]{1,0:T(4,128)}, u32[]{:S(2)}) %copy-start.1) | copy-done | bytes 32792
  2.5 0.0 copy-start.2
  2.5 0.7 %copy-done.2 = s32[2048]{0:T(1024)S(1)} copy-done((s32[2048]{0:T(1024)S(1)}, s32[2048]{0:T(1024)}, u32[]{:S(2)}) %copy-start.2) | copy-done | bytes 8216
  3.2 24.8 %channelize.1.ordered_ref = bf16[128,2048]{1,0:T(8,128)(2,1)S(1)} custom-call(s32[1]{0:T(128)S(6)} %copy.6.start_ref, f32[2,32,2048]{2,1,0:T(8,128)S(1)} %copy-done, f32[4,2048]{1,0:T(4,128)S(1)} %copy-done.1, s32[1,2048]{1,0:T(1,128)S(1)} %bitcast.1, bf16[32768,256]{1,0:T(8,128)(2,1)} %volts_ref.1), custom_call_target="tpu_custom_call" | custom-call | flops 4294967296 | bytes 16777216 | tf_op jit(solution)/shard_map/channelize/pallas_call | solution.py:272
  27.9 8.0 %correlate.1 = bf16[1,2,2048,2048]{3,2,1,0:T(8,128)(2,1)} custom-call(bf16[128,2048]{1,0:T(8,128)(2,1)S(1)} %channelize.1.ordered_ref), custom_call_target="tpu_custom_call" | custom-call | flops 2147483648 | bytes 16777216 | tf_op jit(solution)/shard_map/correlate/pallas_call | solution.py:312
Async XLA Ops:
  0.7 1.0 %copy-start = (f32[2,32,2048]{2,1,0:T(8,128)S(1)}, f32[2,32,2048]{2,1,0:T(8,128)}, u32[]{:S(2)}) copy-start(f32[2,32,2048]{2,1,0:T(8,128)} %constant.4.clone.base_hbm) | copy-start | bytes 1572868
  1.7 0.8 %copy-start.1 = (f32[4,2048]{1,0:T(4,128)S(1)}, f32[4,2048]{1,0:T(4,128)}, u32[]{:S(2)}) copy-start(f32[4,2048]{1,0:T(4,128)} %constant.5.clone.window_hbm) | copy-start | bytes 98308
  2.5 0.7 %copy-start.2 = (s32[2048]{0:T(1024)S(1)}, s32[2048]{0:T(1024)}, u32[]{:S(2)}) copy-start(s32[2048]{0:T(1024)} %param.7) | copy-start | bytes 24580
